TPU v7x, 32 devices: a whole 2x2x4 slice. The times are simulated.
32 devices in a mesh: groups: 2 (over y), block: 4 (over z), rep: 2 (over x), tile: 2 (over core).
Axes of the slice: x: 2, y: 2, z: 4, core: 2. Of those that a mesh axis runs over, the one named last changes fastest.
Arguments:
- visible: int32 [8, 512, 2], P(('groups', 'block'), ('rep', 'tile')), parts along dimension 0, may hold values from 0 to 11, all different within a row; in each aligned block of 128 rows (0 to 127, 128 to 255, ..., all dimensions but the last counted through in order) at most 43 rows name the same one
- bins: int32 [8, 512, 2, 16], P(('groups', 'block'), ('rep', 'tile')), parts along dimension 0, may hold values from 0 to 255, as said below
- ray_code: bfloat16 [8, 512, 128], P(('groups', 'block'), ('rep', 'tile')), parts along dimension 0, may hold values from -6 to 6
- blend: float32 [8, 512, 2], P(('groups', 'block'), ('rep', 'tile')), parts along dimension 0, may hold values from 0.2 to 5
- truth: float32 [3, 8, 512], P(None, ('groups', 'block'), ('rep', 'tile')), parts along dimension 1, may hold values from 0 to 1
- w_in: bfloat16 [12, 144, 512], P('block'), may hold values from -0.75 to 0.75
- w_hid: bfloat16 [12, 512, 512], P('block'), may hold values from -0.375 to 0.375
- w_out: bfloat16 [12, 4, 512], P('block'), may hold values from -0.5 to 0.5
Outputs:
- rendered: float32 [3, 8, 512], P(None, ('groups', 'block'), ('rep', 'tile')), parts along dimension 1
- flip_map: float32 [8, 512], P(('groups', 'block'), ('rep', 'tile')), parts along dimension 0
- psnr: float32 [2], P('groups'), parts along dimension 0
There are 2 independent parts, one for each index of `groups`. A program takes and returns all parts, laid end to end along the dimension named above; an argument that names none is the same for every part. Nothing has to cross between parts.
Inputs may be any that keep to these rules, and one draw needn't show every extreme that they name: `visible`: each pixel names 2 different blocks; among the 128 pixels of one device no block is named by more than 43 pixels, and some block is named by exactly 43. `bins`: sample j of every list lies in [j * 16, (j + 1) * 16), so each list rises.
All inputs are finite; a program needn't handle non-finite values.
Results may differ from a plain program's by a relative error of at most 0.00061.
Values may be sent and summed in bfloat16 or wider, within the bound.
No kernel may reach another device: no remote copies, remote signals or barrier semaphores. Data moves between devices by JAX's collectives and lax.ppermute only.
A program may use at most 64 MiB of HBM per device.

v0:
```python
import functools
import math

import jax
import jax.numpy as jnp
import ml_dtypes
import numpy as np
from jax import lax
from jax.experimental import pallas as pl
from jax.experimental.pallas import tpu as pltpu
from jax.sharding import PartitionSpec as P

RC = 128
DC = 16
NBINS = 256
EXTRA = 16
LISTS = 64

OPPONENT = ((0.2126, 0.7152, 0.0722), (0.5, -0.5, 0.0), (0.0, 0.4, -0.4))
SPREAD = (0.6, 0.35, 0.35)
EMPHASIS = (1.0, 2.0, 2.0)

F32 = jnp.float32
BF16 = jnp.bfloat16


def iota(shape, dim):
    return lax.broadcasted_iota(jnp.int32, shape, dim)


def parts_of(values):
    high = values.astype(BF16).astype(F32)
    rest = values - high
    middle = rest.astype(BF16).astype(F32)
    return [high, middle, rest - middle]


def depth_table(sample_num):
    powers = np.arange(DC // 2, dtype=np.float32)
    steps = (np.float32(np.pi) * np.exp2(powers) / np.float32(NBINS)).astype(np.float32)
    angles = np.arange(NBINS, dtype=np.float32)[:, None] * steps
    wide = angles.astype(np.float64)
    code = np.concatenate([np.sin(wide), np.cos(wide)], axis=1).astype(np.float32)
    stride = NBINS // sample_num
    table = np.zeros((NBINS, sample_num, DC), np.float32)
    for row in range(NBINS):
        table[row, row // stride] = code[row]
    return table.reshape(NBINS, sample_num * DC).astype(ml_dtypes.bfloat16)


def layout_kernel(samples, before, spread, blank):
    before[...] = (iota(before.shape, 0) < iota(before.shape, 1)).astype(F32).astype(BF16)
    row = iota(spread.shape[1:], 0)
    here = row % samples == iota(spread.shape[1:], 1) // DC
    for k in range(spread.shape[0]):
        mine = here & (row % LISTS // samples == k)
        spread[k] = mine.astype(F32).astype(BF16)
    blank[...] = jnp.zeros_like(blank)


def pack_kernel(visible, bins, ray_code, blend, blank, message):
    pixels = ray_code.shape[0]
    listed = bins.shape[0] * bins.shape[1]
    message[0:pixels] = ray_code[...]
    message[pixels : pixels + listed] = bins[...].astype(F32).reshape(listed, pixels).astype(BF16)
    shares = blend[...] / jnp.sum(blend[...], axis=0, keepdims=True)
    rows = [visible[...].astype(F32)] + parts_of(shares) + [blank[...]]
    message[pixels + listed :] = jnp.concatenate(rows, axis=0).astype(BF16)


def tiles_for(most, sizes):
    bounds = [0] + [size for size in sizes if size < most] + [-(-most // 8) * 8]
    return [(high, low, high) for low, high in zip(bounds, bounds[1:])]


def lay_out_weights(samples, w_in, w_out, first_w, last_w):
    local_blocks, in_width, hidden = w_in.shape
    for k in range(local_blocks):
        first_w[k, 0:RC] = w_in[k, 0:RC]
        for i in range(RC // DC):
            first_w[k, RC + i * DC : RC + (i + 1) * DC] = w_in[k, RC:]
        wide = jnp.concatenate(
            [
                jnp.broadcast_to(w_out[k, c : c + 1].astype(F32), (samples, hidden))
                for c in range(4)
            ]
            + [jnp.zeros((128 - 4 * samples, hidden), F32)],
            axis=0,
        )
        last_w[k] = wide.T.astype(BF16)


def serve_kernel(own, sources, slots, tiles, *refs):
    messages = refs[:sources]
    if own:
        aside, w_in, w_hid, w_out, table, before, partial, first_w, last_w = refs[
            sources : sources + 9
        ]
    else:
        aside, first_w, w_hid, last_w, table, before, spread, partial, mixed = refs[
            sources : sources + 9
        ]
    places, codes, depths, heads = refs[-4:]
    local_blocks = w_hid.shape[0]
    pixels = messages[0].shape[1]
    lists = messages[0].shape[0] - pixels - EXTRA
    samples = lists // 2
    if own:
        lay_out_weights(samples, w_in, w_out, first_w, last_w)
    first_block = lax.axis_index("block") * local_blocks

    extras = [messages[s][pixels + lists :].astype(F32) for s in range(sources)]

    named = []
    for s in range(sources):
        block = iota((8, pixels), 0)
        known = (block + first_block).astype(F32)
        named.append(
            [
                ((extras[s][v : v + 1] == known) & (block < local_blocks)).astype(F32)
                for v in range(2)
            ]
        )
    either = [first + second for first, second in named]
    ranks = jnp.dot(
        jnp.concatenate(either, axis=0).astype(BF16), before[...], preferred_element_type=F32
    )
    offset = jnp.zeros((8, 1), F32)
    slot_row = iota((slots, pixels), 0).astype(F32)
    for s in range(sources):
        spot = jnp.where(either[s] > 0.0, ranks[8 * s : 8 * s + 8] + offset, -1.0)
        offset = offset + jnp.sum(either[s], axis=1, keepdims=True)
        for k in range(local_blocks):
            places[k * slots : (k + 1) * slots, s * pixels : (s + 1) * pixels] = (
                (slot_row == spot[k : k + 1]).astype(F32).astype(BF16)
            )
    counts = [jnp.max(offset[k : k + 1]).astype(jnp.int32) for k in range(local_blocks)]

    if own:
        spans = [messages[s][0:pixels] for s in range(sources)]
        codes[...] = jnp.dot(
            places[...], jnp.concatenate(spans, axis=0), preferred_element_type=F32
        ).astype(BF16)
        marks_shape = (samples, DC, pixels)
        mark = (iota(marks_shape, 0) * DC + iota(marks_shape, 1)).astype(F32)
        listed = [messages[s][pixels : pixels + lists].astype(F32) for s in range(sources)]
        for k in range(local_blocks):
            marked = []
            for s in range(sources):
                bins = jnp.where(
                    named[s][0][k : k + 1] > 0.0, listed[s][:samples], listed[s][samples:]
                )
                hit = jnp.broadcast_to(bins[:, None, :], marks_shape) == mark
                marked.append(hit.astype(F32).reshape(samples * DC, pixels).astype(BF16))
            rows = slice(k * slots, (k + 1) * slots)
            is_bin = lax.dot_general(
                places[rows],
                jnp.concatenate(marked, axis=1),
                (((1,), (1,)), ((), ())),
                preferred_element_type=F32,
            ).astype(BF16)
            depths[rows] = jnp.dot(is_bin, table[...], preferred_element_type=F32).astype(BF16)
    else:
        lane = iota((pixels, pixels), 1)
        per_turn = pixels // LISTS
        for turn in range(0, sources, per_turn):
            group = []
            for s in range(turn, min(turn + per_turn, sources)):
                bins = messages[s][pixels : pixels + lists].astype(F32)
                for k in range(local_blocks):
                    group.append(
                        jnp.where(named[s][0][k : k + 1] > 0.0, bins[:samples], bins[samples:])
                    )
                group.append(jnp.zeros((LISTS - local_blocks * samples, pixels), F32))
            rows = sum(part.shape[0] for part in group)
            if rows < pixels:
                group.append(jnp.zeros((pixels - rows, pixels), F32))
            turned = jnp.concatenate(group, axis=0).T
            for s in range(turn, min(turn + per_turn, sources)):
                mixed[s * pixels : (s + 1) * pixels, 0:RC] = messages[s][0:pixels]
                mixed[s * pixels : (s + 1) * pixels, RC:] = jnp.where(
                    lane // LISTS == s - turn, turned, 0.0
                ).astype(BF16)

        chosen = jnp.dot(places[...], mixed[...], preferred_element_type=F32).astype(BF16)
        codes[...] = chosen[:, :RC]
        bins = jnp.concatenate(
            [
                jnp.dot(
                    chosen[k * slots : (k + 1) * slots, RC:], spread[k], preferred_element_type=F32
                )
                for k in range(local_blocks)
            ],
            axis=0,
        )
        is_bin = (bins == iota(bins.shape, 1).astype(F32)).astype(F32).astype(BF16)
        depths[...] = jnp.dot(is_bin, table[...], preferred_element_type=F32).astype(BF16)

    heads[...] = jnp.zeros_like(heads)
    per_half = RC // DC
    def one_block(k, carry):
        count = carry[0]
        for i in range(1, local_blocks):
            count = jnp.where(k == i, carry[i], count)

        def one_tile(start, size):
            rows = pl.ds(pl.multiple_of(k * slots + start, 16), -(-size // 16) * 16)
            code = codes[rows, :]
            depth = depths[rows, :]
            if size % 16:
                code = code.astype(F32)[:size]
                depth = depth.astype(F32)[:size]
            half_lane = iota((size, RC), 1) // DC
            inputs = []
            for j in range(samples):
                half = depth[:, (j // per_half) * RC : (j // per_half + 1) * RC]
                kept = jnp.where(half_lane == j % per_half, half, jnp.zeros_like(half))
                inputs.append(jnp.concatenate([code, kept], axis=1))
            inputs = jnp.concatenate(inputs, axis=0).astype(BF16)
            one = jnp.dot(inputs, first_w[k], preferred_element_type=F32)
            one = jnp.maximum(one, 0.0).astype(BF16)
            two = jnp.dot(one, w_hid[k], preferred_element_type=F32)
            two = jnp.maximum(two, 0.0).astype(BF16)
            out = jnp.dot(two, last_w[k], preferred_element_type=F32)
            sample_lane = iota((size, 128), 1) % samples
            total = jnp.zeros((size, 128), F32)
            for j in range(samples):
                total = jnp.where(sample_lane == j, out[j * size : (j + 1) * size], total)
            heads[pl.ds(pl.multiple_of(k * slots + start, 16), size), :] = total

        def pick(choices):
            if len(choices) == 1:
                one_tile(0, choices[0][0])
                return
            half = len(choices) // 2
            bound = choices[half - 1][2]

            @pl.when(count <= bound)
            def _():
                pick(choices[:half])

            @pl.when(count > bound)
            def _():
                pick(choices[half:])

        @pl.when(count > 0)
        def _():
            pick(tiles)

        return carry

    lax.fori_loop(0, local_blocks, one_block, tuple(counts))

    turned = heads[...].T
    optical = jax.nn.softplus(turned[0:samples]) * (1.5 / samples)
    sample_row = iota(optical.shape, 0)
    ahead = jnp.where(sample_row >= 1, pltpu.roll(optical, 1, 0), 0.0)
    step = 1
    while step < samples:
        ahead = ahead + jnp.where(sample_row >= step, pltpu.roll(ahead, step, 0), 0.0)
        step = 2 * step
    weights = jnp.exp(-ahead) * (1.0 - jnp.exp(-optical))
    background = 1.0 - jnp.sum(weights, axis=0, keepdims=True)
    shades = []
    for c in range(1, 4):
        color = jax.nn.sigmoid(turned[c * samples : (c + 1) * samples])
        shades.append(jnp.sum(weights * color, axis=0, keepdims=True) + background)
    shades.append(jnp.zeros_like(background))
    shades = jnp.concatenate(shades, axis=0)[:, : local_blocks * slots]
    stacked = jnp.concatenate(parts_of(shades) + [jnp.zeros_like(shades)], axis=0).astype(BF16)
    sums = [jnp.zeros((3, pixels), F32)] * sources
    for k in range(local_blocks):
        spots = jnp.dot(
            stacked[:, k * slots : (k + 1) * slots],
            places[k * slots : (k + 1) * slots],
            preferred_element_type=F32,
        )
        spots = spots[0:4] + spots[4:8] + spots[8:12]
        for s in range(sources):
            share = jnp.zeros((1, pixels), F32)
            for v in range(2):
                part = extras[s][2 + v : 3 + v] + extras[s][4 + v : 5 + v] + extras[s][6 + v : 7 + v]
                share = share + named[s][v][k : k + 1] * part
            sums[s] = sums[s] + spots[0:3, s * pixels : (s + 1) * pixels] * share
    if own:
        partial[...] = sums[0] - aside[...].reshape(3, pixels)
    else:
        partial[...] = jnp.concatenate([aside[...]] + sums, axis=0)


def gather_kernel(sources, *refs):
    partials = refs[:sources]
    (message,) = refs[sources:]
    pixels = message.shape[1]
    z = lax.axis_index("block")
    squared = jnp.zeros((3, pixels), F32)
    rows = []
    for u in range(sources):
        difference = partials[0][3 * u : 3 * u + 3]
        for t in range(1, sources):
            difference = difference + partials[t][3 * (t ^ u) : 3 * (t ^ u) + 3]
        squared = squared + difference * difference
        rows.append(difference)
    above = jnp.zeros((3, pixels), F32)
    below = jnp.zeros((3, pixels), F32)
    for u in range(1, sources):
        above = above + jnp.where((z ^ u) == z - 1, rows[u], 0.0)
        below = below + jnp.where((z ^ u) == z + 1, rows[u], 0.0)

    def opponent(block, c):
        return sum(OPPONENT[c][i] * block[i : i + 1] for i in range(3) if OPPONENT[c][i])

    mixed = [
        SPREAD[c] * opponent(above, c) + opponent(rows[0], c) + SPREAD[c] * opponent(below, c)
        for c in range(3)
    ]
    total = jnp.sum(jnp.sum(squared, axis=0, keepdims=True), axis=1, keepdims=True)
    message[...] = jnp.concatenate(
        mixed + [jnp.broadcast_to(total, (1, pixels)), rows[0]], axis=0
    )


def finish_kernel(columns, count, *refs):
    messages = refs[:columns]
    truth, rendered, flip_map, psnr = refs[columns:]
    pixels = flip_map.shape[1]
    q = lax.axis_index("rep") * lax.axis_size("tile") + lax.axis_index("tile")
    rendered[...] = messages[0][4:7].reshape(3, 1, pixels) + truth[...]
    own = messages[0][0:4]
    left = jnp.zeros_like(own)
    right = jnp.zeros_like(own)
    total = own[3:4]
    for s in range(1, columns):
        other = messages[s][0:4]
        left = left + jnp.where((q ^ s) == q - 1, other, 0.0)
        right = right + jnp.where((q ^ s) == q + 1, other, 0.0)
        total = total + other[3:4]
    lane = iota(own.shape, 1)
    before = pltpu.roll(jnp.where(lane == pixels - 1, left, own), 1, 1)
    after = pltpu.roll(jnp.where(lane == 0, right, own), pixels - 1, 1)
    summed = jnp.zeros((1, pixels), F32)
    for c in range(3):
        column = SPREAD[c] * before[c : c + 1] + own[c : c + 1] + SPREAD[c] * after[c : c + 1]
        scale = np.float32(1.0) + np.float32(2.0) * np.float32(SPREAD[c])
        emphasised = EMPHASIS[c] * (column / float(scale * scale))
        summed = summed + emphasised * emphasised
    flip_map[...] = jnp.sqrt(summed + 1e-06)
    logged = jnp.log(total / count + 1e-06) * (-10.0 / math.log(10.0))
    psnr[...] = logged[:, 0:1]


def exchange(value, axes, size):
    out = [value]
    for s in range(1, size):
        out.append(lax.ppermute(value, axes, [(i, i ^ s) for i in range(size)]))
    return out


def call(
    kernel, out_shape, in_specs, scratch, flops=0, bytes_accessed=0, limit=8 << 20
):
    cost = None
    if flops:
        cost = pl.CostEstimate(flops=flops, bytes_accessed=bytes_accessed, transcendentals=0)
    return pl.pallas_call(
        kernel,
        out_shape=out_shape,
        in_specs=in_specs,
        scratch_shapes=list(scratch),
        cost_estimate=cost,
        compiler_params=pltpu.CompilerParams(vmem_limit_bytes=limit),
    )


def body(visible, bins, ray_code, blend, truth, w_in, w_hid, w_out):
    sources = lax.axis_size("block")
    columns = lax.axis_size("rep") * lax.axis_size("tile")
    local_blocks, in_width, hidden = w_in.shape
    pixels = visible.shape[1]
    visible_num = visible.shape[2]
    samples = bins.shape[3]
    blocks_all = local_blocks * sources
    capacity = (2 * pixels * visible_num + blocks_all - 1) // blocks_all
    lists = visible_num * samples
    height = pixels + lists + EXTRA
    far = pl.BlockSpec(memory_space=pltpu.HBM)
    near = pl.BlockSpec(memory_space=pltpu.VMEM)
    before, spread, blank = call(
        functools.partial(layout_kernel, samples),
        (
            jax.ShapeDtypeStruct((pixels, pixels), BF16),
            jax.ShapeDtypeStruct((local_blocks, pixels, samples * DC), BF16),
            jax.ShapeDtypeStruct((EXTRA - 4 * visible_num, pixels), F32),
        ),
        [],
        (),
        flops=1 << 32,
        bytes_accessed=1 << 17,
    )()
    message = call(
        pack_kernel,
        jax.ShapeDtypeStruct((height, pixels), BF16),
        [near] * 5,
        (),
        flops=1 << 32,
        bytes_accessed=1 << 17,
    )(
        visible.reshape(pixels, visible_num).T,
        jnp.transpose(bins.reshape(pixels, visible_num, samples), (1, 2, 0)),
        ray_code.reshape(pixels, RC),
        blend.reshape(pixels, visible_num).T,
        blank,
    )
    messages = exchange(message, "block", sources)
    table = jnp.asarray(depth_table(samples))

    def serve(own, parts, aside, weights):
        count = len(parts)
        slots = -(-count * capacity // 16) * 16
        slots_all = local_blocks * slots
        outs = [jax.ShapeDtypeStruct((3 * count + 3 * (not own), pixels), F32)]
        if own:
            outs.append(jax.ShapeDtypeStruct((local_blocks, 2 * RC, hidden), BF16))
            outs.append(jax.ShapeDtypeStruct((local_blocks, hidden, 128), BF16))
        return call(
            functools.partial(
                serve_kernel, own, count, slots, tiles_for(count * capacity, list(range(8, slots, 8)))
            ),
            outs,
            [near] * (count + 6 + (not own)),
            ([] if own else [pltpu.VMEM((count * pixels, 2 * RC), BF16)])
            + [
                pltpu.VMEM((slots_all, count * pixels), BF16),
                pltpu.VMEM((slots_all, RC), BF16),
                pltpu.VMEM((slots_all, samples * DC), BF16),
                pltpu.VMEM((-(-slots_all // 128) * 128, 128), F32),
            ],
            flops=2 * slots_all * samples * hidden * (in_width + hidden + 4),
            bytes_accessed=2 * (w_in.size + w_hid.size),
            limit=40 * 1024 * 1024,
        )(*parts, aside, *weights, table, before, *([] if own else [spread]))

    share, first_w, last_w = serve(True, messages[:1], truth, (w_in, w_hid, w_out))
    (partial,) = serve(False, messages[1:], share, (first_w, w_hid, last_w))
    partials = exchange(partial, "block", sources)
    edge = call(
        functools.partial(gather_kernel, sources),
        jax.ShapeDtypeStruct((7, pixels), F32),
        [near] * sources,
        (),
    )(*partials)
    edges = exchange(edge, ("rep", "tile"), columns)
    rendered, flip_map, psnr = call(
        functools.partial(finish_kernel, columns, 3 * sources * columns * pixels),
        (
            jax.ShapeDtypeStruct((3, 1, pixels), F32),
            jax.ShapeDtypeStruct((1, pixels), F32),
            jax.ShapeDtypeStruct((1, 1), F32),
        ),
        [near] * (columns + 1),
        (),
    )(*edges, truth)
    return (rendered, flip_map, psnr.reshape(1))


def solution(mesh):
    placed = (
        P(("groups", "block"), ("rep", "tile"), None),
        P(("groups", "block"), ("rep", "tile"), None, None),
        P(("groups", "block"), ("rep", "tile"), None),
        P(("groups", "block"), ("rep", "tile"), None),
        P(None, ("groups", "block"), ("rep", "tile")),
        P("block", None, None),
        P("block", None, None),
        P("block", None, None),
    )
    return jax.shard_map(
        body,
        mesh=mesh,
        in_specs=placed,
        out_specs=(
            P(None, ("groups", "block"), ("rep", "tile")),
            P(("groups", "block"), ("rep", "tile")),
            P("groups"),
        ),
        check_vma=False,
    )
```

profile of v0, /device:TPU:0, one launch (start us, length us, event | category | flops | bytes accessed | tf_op | source)
XLA Modules:
  0.0 29.2 jit_solution(12975107409380388771)
XLA Ops:
  0.6 0.0 copy-start.7
  0.6 0.0 copy-start.3
  0.7 0.0 copy-start.4
  0.7 0.0 copy-start.6
  0.7 0.6 %copy-done.7 = f32[1,128,2]{1,2,0:T(2,128)S(1)} copy-done((f32[1,128,2]{1,2,0:T(2,128)S(1)}, f32[1,128,2]{1,2,0:T(2,128)}, u32[]{:S(2)}) %copy-start.7) | copy-done | bytes 1048
  1.3 0.1 copy-done.3
  1.4 0.0 copy-done.4
  1.4 0.0 copy-done.6
  1.4 0.0 copy-start
  1.4 0.0 copy-start.1
  1.4 0.0 copy-start.2
  1.4 0.0 copy-start.5
  1.4 0.0 copy-start.8
  1.5 5.1 %collective-permute-start.2 = (bf16[176,128]{1,0:T(8,128)(2,1)S(1)}, bf16[176,128]{1,0:T(8,128)(2,1)S(1)}, u32[]{:S(2)}, u32[]{:S(2)}) collective-permute-start(bf16[176,128]{1,0:T(8,128)(2,1)S(1)} %shard_map.113.refs_0_), channel_id=1, source_target_pairs={{0,12},{4,8},{8,4},{12,0},{1,13},{5,9},{9,5},{13,1},{2,14},{6,10},... | collective-permute-start | bytes 135176 | tf_op jit(solution)/shard_map/ppermute | solution.py:355
  6.6 0.0 collective-permute-start.1
  6.6 0.6 %collective-permute-start = (bf16[176,128]{1,0:T(8,128)(2,1)S(1)}, bf16[176,128]{1,0:T(8,128)(2,1)S(1)}, u32[]{:S(2)}, u32[]{:S(2)}) collective-permute-start(bf16[176,128]{1,0:T(8,128)(2,1)S(1)} %shard_map.113.refs_0_), channel_id=1, source_target_pairs={{0,4},{4,0},{8,12},{12,8},{1,5},{5,1},{9,13},{13,9},{2,6},{6,2},{1... | collective-permute-start | bytes 135176 | tf_op jit(solution)/shard_map/ppermute | solution.py:355
  7.2 0.0 copy-done
  7.2 0.0 copy-done.1
  7.2 0.0 copy-done.2
  7.2 0.0 copy-done.5
  7.3 0.0 copy-done.8
  7.3 3.0 %shard_map.114 = (f32[3,128]{1,0:T(4,128)S(1)}, bf16[3,256,512]{2,1,0:T(8,128)(2,1)S(1)}, bf16[3,512,128]{2,1,0:T(8,128)(2,1)S(1)}) custom-call(bf16[176,128]{1,0:T(8,128)(2,1)S(1)} %shard_map.113.refs_0_, f32[3,1,128]{2,1,0:T(1,128)S(1)} %copy-done, bf16[3,144,512]{2,1,0:T(8,128)(2,1)S(1)} %copy-done.2, bf16[3,512,512]{2,1,0:T(8,128)(2,1)S(1)} %copy-done.1, ...), custom_call_target="tpu_custom_call" | custom-call | flops 1557135360 | bytes 2015232 | tf_op jit(solution)/shard_map/pallas_call | solution.py:425
  10.2 0.0 collective-permute-done.2.refs_2_
  10.2 1.3 %collective-permute-done.1.refs_1_ = bf16[176,128]{1,0:T(8,128)(2,1)S(1)} collective-permute-done((bf16[176,128]{1,0:T(8,128)(2,1)S(1)}, bf16[176,128]{1,0:T(8,128)(2,1)S(1)}, u32[]{:S(2)}, u32[]{:S(2)}) %collective-permute-start.1) | collective-permute-done | bytes 45088 | tf_op jit(solution)/shard_map/ppermute | solution.py:355
  11.5 0.0 collective-permute-done.refs_0_
  11.5 5.7 %shard_map.115.refs_0_ = f32[12,128]{1,0:T(8,128)S(1)} custom-call(bf16[176,128]{1,0:T(8,128)(2,1)S(1)} %collective-permute-done.refs_0_, bf16[176,128]{1,0:T(8,128)(2,1)S(1)} %collective-permute-done.1.refs_1_, bf16[176,128]{1,0:T(8,128)(2,1)S(1)} %collective-permute-done.2.refs_2_, f32[3,128]{1,0:T(4,128)S(1)} %get-tuple-element.14.refs_3_, ...), custom_call_target="tpu_custom_call" | custom-call | flops 4671406080 | bytes 2015232 | tf_op jit(solution)/shard_map/pallas_call | solution.py:425
  17.3 3.0 %collective-permute-start.5 = (f32[12,128]{1,0:T(8,128)S(1)}, f32[12,128]{1,0:T(8,128)S(1)}, u32[]{:S(2)}, u32[]{:S(2)}) collective-permute-start(f32[12,128]{1,0:T(8,128)S(1)} %shard_map.115.refs_0_), channel_id=1, source_target_pairs={{0,12},{4,8},{8,4},{12,0},{1,13},{5,9},{9,5},{13,1},{2,14},{6,10},... | collective-permute-start | bytes 18440 | tf_op jit(solution)/shard_map/ppermute | solution.py:355
  20.2 0.0 collective-permute-start.4
  20.2 1.5 %collective-permute-start.3 = (f32[12,128]{1,0:T(8,128)S(1)}, f32[12,128]{1,0:T(8,128)S(1)}, u32[]{:S(2)}, u32[]{:S(2)}) collective-permute-start(f32[12,128]{1,0:T(8,128)S(1)} %shard_map.115.refs_0_), channel_id=1, source_target_pairs={{0,4},{4,0},{8,12},{12,8},{1,5},{5,1},{9,13},{13,9},{2,6},{6,2},{1... | collective-permute-start | bytes 18440 | tf_op jit(solution)/shard_map/ppermute | solution.py:355
  21.7 1.1 %collective-permute-done.5.refs_3_ = f32[12,128]{1,0:T(8,128)S(1)} collective-permute-done((f32[12,128]{1,0:T(8,128)S(1)}, f32[12,128]{1,0:T(8,128)S(1)}, u32[]{:S(2)}, u32[]{:S(2)}) %collective-permute-start.5) | collective-permute-done | bytes 6176 | tf_op jit(solution)/shard_map/ppermute | solution.py:355
  22.8 2.0 %collective-permute-done.4.refs_2_ = f32[12,128]{1,0:T(8,128)S(1)} collective-permute-done((f32[12,128]{1,0:T(8,128)S(1)}, f32[12,128]{1,0:T(8,128)S(1)}, u32[]{:S(2)}, u32[]{:S(2)}) %collective-permute-start.4) | collective-permute-done | bytes 6176 | tf_op jit(solution)/shard_map/ppermute | solution.py:355
  24.8 0.0 collective-permute-done.3.refs_1_
  24.8 0.1 shard_map.116.refs_0_
  24.9 0.0 collective-permute-start.8
  24.9 1.3 %collective-permute-start.7 = (f32[7,128]{1,0:T(8,128)S(1)}, f32[7,128]{1,0:T(8,128)S(1)}, u32[]{:S(2)}, u32[]{:S(2)}) collective-permute-start(f32[7,128]{1,0:T(8,128)S(1)} %shard_map.116.refs_0_), channel_id=1, source_target_pairs={{0,2},{1,3},{2,0},{3,1},{4,6},{5,7},{6,4},{7,5},{8,10},{9,11},{10,... | collective-permute-start | bytes 10760 | tf_op jit(solution)/shard_map/ppermute | solution.py:355
  26.2 0.6 %collective-permute-start.6 = (f32[7,128]{1,0:T(8,128)S(1)}, f32[7,128]{1,0:T(8,128)S(1)}, u32[]{:S(2)}, u32[]{:S(2)}) collective-permute-start(f32[7,128]{1,0:T(8,128)S(1)} %shard_map.116.refs_0_), channel_id=1, source_target_pairs={{0,1},{1,0},{2,3},{3,2},{4,5},{5,4},{6,7},{7,6},{8,9},{9,8},{10,11... | collective-permute-start | bytes 10760 | tf_op jit(solution)/shard_map/ppermute | solution.py:355
  26.7 1.2 %collective-permute-done.8.refs_3_ = f32[7,128]{1,0:T(8,128)S(1)} collective-permute-done((f32[7,128]{1,0:T(8,128)S(1)}, f32[7,128]{1,0:T(8,128)S(1)}, u32[]{:S(2)}, u32[]{:S(2)}) %collective-permute-start.8) | collective-permute-done | bytes 3616 | tf_op jit(solution)/shard_map/ppermute | solution.py:355
  27.9 0.7 %collective-permute-done.7.refs_2_ = f32[7,128]{1,0:T(8,128)S(1)} collective-permute-done((f32[7,128]{1,0:T(8,128)S(1)}, f32[7,128]{1,0:T(8,128)S(1)}, u32[]{:S(2)}, u32[]{:S(2)}) %collective-permute-start.7) | collective-permute-done | bytes 3616 | tf_op jit(solution)/shard_map/ppermute | solution.py:355
  28.6 0.0 collective-permute-done.6.refs_1_
  28.6 0.6 %shard_map.117 = (f32[3,1,128]{2,1,0:T(1,128)}, f32[1,128]{1,0:T(1,128)}, f32[1,1]{1,0:T(1,128)}) custom-call(f32[7,128]{1,0:T(8,128)S(1)} %shard_map.116.refs_0_, f32[7,128]{1,0:T(8,128)S(1)} %collective-permute-done.6.refs_1_, f32[7,128]{1,0:T(8,128)S(1)} %collective-permute-done.7.refs_2_, f32[7,128]{1,0:T(8,128)S(1)} %collective-permute-done.8.refs_3_, ...), custom_call_target="tpu_custom_call" | custom-call | tf_op jit(solution)/shard_map/pallas_call | solution.py:453
  (2 shorter events, 0.1 us)
Async XLA Ops:
  0.6 0.7 %copy-start.7 = (f32[1,128,2]{1,2,0:T(2,128)S(1)}, f32[1,128,2]{1,2,0:T(2,128)}, u32[]{:S(2)}) copy-start(f32[1,128,2]{1,2,0:T(2,128)} %param.12) | copy-start | bytes 3076
  0.6 0.8 %copy-start.3 = (bf16[1,128,128]{2,1,0:T(8,128)(2,1)S(1)}, bf16[1,128,128]{2,1,0:T(8,128)(2,1)}, u32[]{:S(2)}) copy-start(bf16[1,128,128]{2,1,0:T(8,128)(2,1)} %param.11) | copy-start | bytes 98308
  0.7 0.8 %copy-start.4 = (s32[1,128,2,16]{1,3,2,0:T(8,128)S(1)}, s32[1,128,2,16]{1,3,2,0:T(8,128)}, u32[]{:S(2)}) copy-start(s32[1,128,2,16]{1,3,2,0:T(8,128)} %param.10) | copy-start | bytes 49156
  0.7 0.8 %copy-start.6 = (s32[1,128,2]{1,2,0:T(2,128)S(1)}, s32[1,128,2]{1,2,0:T(2,128)}, u32[]{:S(2)}) copy-start(s32[1,128,2]{1,2,0:T(2,128)} %param.9) | copy-start | bytes 3076
  1.4 5.8 %copy-start = (f32[3,1,128]{2,1,0:T(1,128)S(1)}, f32[3,1,128]{2,1,0:T(1,128)}, u32[]{:S(2)}) copy-start(f32[3,1,128]{2,1,0:T(1,128)} %refs_4_.3) | copy-start | bytes 4612
  1.4 5.8 %copy-start.1 = (bf16[3,512,512]{2,1,0:T(8,128)(2,1)S(1)}, bf16[3,512,512]{2,1,0:T(8,128)(2,1)}, u32[]{:S(2)}) copy-start(bf16[3,512,512]{2,1,0:T(8,128)(2,1)} %refs_5_.2) | copy-start | bytes 4718596
  1.4 5.8 %copy-start.2 = (bf16[3,144,512]{2,1,0:T(8,128)(2,1)S(1)}, bf16[3,144,512]{2,1,0:T(8,128)(2,1)}, u32[]{:S(2)}) copy-start(bf16[3,144,512]{2,1,0:T(8,128)(2,1)} %refs_2_.1) | copy-start | bytes 1327108
  1.4 5.8 %copy-start.5 = (bf16[3,4,512]{2,1,0:T(4,128)(2,1)S(1)}, bf16[3,4,512]{2,1,0:T(4,128)(2,1)}, u32[]{:S(2)}) copy-start(bf16[3,4,512]{2,1,0:T(4,128)(2,1)} %refs_4_.2) | copy-start | bytes 36868
  1.4 5.8 %copy-start.8 = (bf16[256,256]{1,0:T(8,128)(2,1)S(1)}, bf16[256,256]{1,0:T(8,128)(2,1)}, u32[]{:S(2)}) copy-start(bf16[256,256]{1,0:T(8,128)(2,1)} %constant.2.clone.refs_5_.refs_7_) | copy-start | bytes 393220
  1.5 8.7 %collective-permute-start.2 = (bf16[176,128]{1,0:T(8,128)(2,1)S(1)}, bf16[176,128]{1,0:T(8,128)(2,1)S(1)}, u32[]{:S(2)}, u32[]{:S(2)}) collective-permute-start(bf16[176,128]{1,0:T(8,128)(2,1)S(1)} %shard_map.113.refs_0_), channel_id=1, source_target_pairs={{0,12},{4,8},{8,4},{12,0},{1,13},{5,9},{9,5},{13,1},{2,14},{6,10},... | collective-permute-start | bytes 135176 | tf_op jit(solution)/shard_map/ppermute | solution.py:355
  6.6 4.9 %collective-permute-start.1 = (bf16[176,128]{1,0:T(8,128)(2,1)S(1)}, bf16[176,128]{1,0:T(8,128)(2,1)S(1)}, u32[]{:S(2)}, u32[]{:S(2)}) collective-permute-start(bf16[176,128]{1,0:T(8,128)(2,1)S(1)} %shard_map.113.refs_0_), channel_id=1, source_target_pairs={{0,8},{4,12},{8,0},{12,4},{1,9},{5,13},{9,1},{13,5},{2,10},{6,14},... | collective-permute-start | bytes 135176 | tf_op jit(solution)/shard_map/ppermute | solution.py:355
  6.6 4.9 %collective-permute-start = (bf16[176,128]{1,0:T(8,128)(2,1)S(1)}, bf16[176,128]{1,0:T(8,128)(2,1)S(1)}, u32[]{:S(2)}, u32[]{:S(2)}) collective-permute-start(bf16[176,128]{1,0:T(8,128)(2,1)S(1)} %shard_map.113.refs_0_), channel_id=1, source_target_pairs={{0,4},{4,0},{8,12},{12,8},{1,5},{5,1},{9,13},{13,9},{2,6},{6,2},{1... | collective-permute-start | bytes 135176 | tf_op jit(solution)/shard_map/ppermute | solution.py:355
  17.3 5.5 %collective-permute-start.5 = (f32[12,128]{1,0:T(8,128)S(1)}, f32[12,128]{1,0:T(8,128)S(1)}, u32[]{:S(2)}, u32[]{:S(2)}) collective-permute-start(f32[12,128]{1,0:T(8,128)S(1)} %shard_map.115.refs_0_), channel_id=1, source_target_pairs={{0,12},{4,8},{8,4},{12,0},{1,13},{5,9},{9,5},{13,1},{2,14},{6,10},... | collective-permute-start | bytes 18440 | tf_op jit(solution)/shard_map/ppermute | solution.py:355
  20.2 4.5 %collective-permute-start.4 = (f32[12,128]{1,0:T(8,128)S(1)}, f32[12,128]{1,0:T(8,128)S(1)}, u32[]{:S(2)}, u32[]{:S(2)}) collective-permute-start(f32[12,128]{1,0:T(8,128)S(1)} %shard_map.115.refs_0_), channel_id=1, source_target_pairs={{0,8},{4,12},{8,0},{12,4},{1,9},{5,13},{9,1},{13,5},{2,10},{6,14},... | collective-permute-start | bytes 18440 | tf_op jit(solution)/shard_map/ppermute | solution.py:355
  20.2 4.5 %collective-permute-start.3 = (f32[12,128]{1,0:T(8,128)S(1)}, f32[12,128]{1,0:T(8,128)S(1)}, u32[]{:S(2)}, u32[]{:S(2)}) collective-permute-start(f32[12,128]{1,0:T(8,128)S(1)} %shard_map.115.refs_0_), channel_id=1, source_target_pairs={{0,4},{4,0},{8,12},{12,8},{1,5},{5,1},{9,13},{13,9},{2,6},{6,2},{1... | collective-permute-start | bytes 18440 | tf_op jit(solution)/shard_map/ppermute | solution.py:355
  24.9 3.0 %collective-permute-start.8 = (f32[7,128]{1,0:T(8,128)S(1)}, f32[7,128]{1,0:T(8,128)S(1)}, u32[]{:S(2)}, u32[]{:S(2)}) collective-permute-start(f32[7,128]{1,0:T(8,128)S(1)} %shard_map.116.refs_0_), channel_id=1, source_target_pairs={{0,3},{1,2},{2,1},{3,0},{4,7},{5,6},{6,5},{7,4},{8,11},{9,10},{10,... | collective-permute-start | bytes 10760 | tf_op jit(solution)/shard_map/ppermute | solution.py:355
  24.9 3.7 %collective-permute-start.7 = (f32[7,128]{1,0:T(8,128)S(1)}, f32[7,128]{1,0:T(8,128)S(1)}, u32[]{:S(2)}, u32[]{:S(2)}) collective-permute-start(f32[7,128]{1,0:T(8,128)S(1)} %shard_map.116.refs_0_), channel_id=1, source_target_pairs={{0,2},{1,3},{2,0},{3,1},{4,6},{5,7},{6,4},{7,5},{8,10},{9,11},{10,... | collective-permute-start | bytes 10760 | tf_op jit(solution)/shard_map/ppermute | solution.py:355
  26.2 2.4 %collective-permute-start.6 = (f32[7,128]{1,0:T(8,128)S(1)}, f32[7,128]{1,0:T(8,128)S(1)}, u32[]{:S(2)}, u32[]{:S(2)}) collective-permute-start(f32[7,128]{1,0:T(8,128)S(1)} %shard_map.116.refs_0_), channel_id=1, source_target_pairs={{0,1},{1,0},{2,3},{3,2},{4,5},{5,4},{6,7},{7,6},{8,9},{9,8},{10,11... | collective-permute-start | bytes 10760 | tf_op jit(solution)/shard_map/ppermute | solution.py:355
where the time goes:
time: 29.5 us; the launch traced here: 29.2 us
  starting transfers between devices  12.1 us (41%)
  Pallas kernels  9.43 us (32%)
  waiting for transfers between devices  6.21 us (21%)
  local copies, waits for them, and re-layouts  0.74 us (3%)
  between operations  0.74 us (3%)
    ppermute x9, starting transfers between devices, exchange(): out.append(lax.ppermute(value, axes, [(i, i ^ s) for i in range(size)]))  12.1 us
    pallas_call x2, Pallas kernels, serve(): call(functools.partial(serve_kernel, own, count, slots, tiles_for(count *...  8.66 us
    ppermute x9, waiting for transfers between devices, exchange(): out.append(lax.ppermute(value, axes, [(i, i ^ s) for i in range(size)]))  6.21 us
    unnamed x18, local copies, waits for them, and re-layouts  0.74 us
    pallas_call x1, Pallas kernels, body(): call(functools.partial(finish_kernel, columns, 3 * sources * columns * pi...  0.62 us
  transfers between devices with their start and end apart: 9, of which 5 were waited for; matrix products, arithmetic and copies ran while one was open for 0% of the time, Pallas kernels for 10%

commit v1 on v0

--- a/solution.py
+++ b/solution.py
@@ -290,7 +290,7 @@
 
 def gather_kernel(sources, *refs):
     partials = refs[:sources]
-    (message,) = refs[sources:]
+    message, errors = refs[sources:]
     pixels = message.shape[1]
     z = lax.axis_index("block")
     squared = jnp.zeros((3, pixels), F32)
@@ -315,23 +315,22 @@
         for c in range(3)
     ]
     total = jnp.sum(jnp.sum(squared, axis=0, keepdims=True), axis=1, keepdims=True)
-    message[...] = jnp.concatenate(
-        mixed + [jnp.broadcast_to(total, (1, pixels)), rows[0]], axis=0
-    )
+    message[...] = jnp.concatenate(mixed + [jnp.broadcast_to(total, (1, pixels))], axis=0)
+    errors[...] = rows[0]
 
 
 def finish_kernel(columns, count, *refs):
     messages = refs[:columns]
-    truth, rendered, flip_map, psnr = refs[columns:]
+    errors, truth, rendered, flip_map, psnr = refs[columns:]
     pixels = flip_map.shape[1]
     q = lax.axis_index("rep") * lax.axis_size("tile") + lax.axis_index("tile")
-    rendered[...] = messages[0][4:7].reshape(3, 1, pixels) + truth[...]
-    own = messages[0][0:4]
+    rendered[...] = errors[...].reshape(3, 1, pixels) + truth[...]
+    own = messages[0][...]
     left = jnp.zeros_like(own)
     right = jnp.zeros_like(own)
     total = own[3:4]
     for s in range(1, columns):
-        other = messages[s][0:4]
+        other = messages[s][...]
         left = left + jnp.where((q ^ s) == q - 1, other, 0.0)
         right = right + jnp.where((q ^ s) == q + 1, other, 0.0)
         total = total + other[3:4]
@@ -443,9 +442,12 @@
     share, first_w, last_w = serve(True, messages[:1], truth, (w_in, w_hid, w_out))
     (partial,) = serve(False, messages[1:], share, (first_w, w_hid, last_w))
     partials = exchange(partial, "block", sources)
-    edge = call(
+    edge, errors = call(
         functools.partial(gather_kernel, sources),
-        jax.ShapeDtypeStruct((7, pixels), F32),
+        (
+            jax.ShapeDtypeStruct((4, pixels), F32),
+            jax.ShapeDtypeStruct((3, pixels), F32),
+        ),
         [near] * sources,
         (),
     )(*partials)
@@ -457,9 +459,9 @@
             jax.ShapeDtypeStruct((1, pixels), F32),
             jax.ShapeDtypeStruct((1, 1), F32),
         ),
-        [near] * (columns + 1),
+        [near] * (columns + 2),
         (),
-    )(*edges, truth)
+    )(*edges, errors, truth)
     return (rendered, flip_map, psnr.reshape(1))
 
 

time: 29.5 us -> 29.5 us (level)
  Pallas kernels: 9.43 us -> 8.27 us
  waiting for transfers between devices: 6.21 us -> 7.23 us
    pallas_call x2, Pallas kernels: 8.66 us -> 7.5 us  [serve(): call(functools.partial(serve_kernel, own, count, slots, tiles_for(count *...]
    ppermute x9, waiting for transfers between devices: 6.21 us -> 7.23 us  [exchange(): out.append(lax.ppermute(value, axes, [(i, i ^ s) for i in range(size)]))]
  transfers between devices with their start and end apart: 9 -> 9, of which waited for: 5 -> 5; matrix products, arithmetic and copies ran while one was open for 0% -> 0% of each run, Pallas kernels for 10% -> 9%
where the time goes in v1:
time: 29.5 us; the launch traced here: 29.2 us
  starting transfers between devices  12.2 us (41%)
  Pallas kernels  8.27 us (28%)
  waiting for transfers between devices  7.23 us (25%)
  local copies, waits for them, and re-layouts  0.74 us (3%)
  between operations  0.74 us (3%)
    ppermute x9, starting transfers between devices, exchange(): out.append(lax.ppermute(value, axes, [(i, i ^ s) for i in range(size)]))  12.2 us
    pallas_call x2, Pallas kernels, serve(): call(functools.partial(serve_kernel, own, count, slots, tiles_for(count *...  7.5 us
    ppermute x9, waiting for transfers between devices, exchange(): out.append(lax.ppermute(value, axes, [(i, i ^ s) for i in range(size)]))  7.23 us
    unnamed x18, local copies, waits for them, and re-layouts  0.74 us
    pallas_call x1, Pallas kernels, body(): call(functools.partial(finish_kernel, columns, 3 * sources * columns * pi...  0.62 us
  transfers between devices with their start and end apart: 9, of which 5 were waited for; matrix products, arithmetic and copies ran while one was open for 0% of the time, Pallas kernels for 9%

profile of v1, /device:TPU:0, one launch (start us, length us, event | category | flops | bytes accessed | tf_op | source)
XLA Modules:
  0.0 29.2 jit_solution(18086568309743037253)
XLA Ops:
  0.6 0.0 copy-start.7
  0.6 0.0 copy-start.3
  0.7 0.0 copy-start.4
  0.7 0.0 copy-start.6
  0.7 0.6 %copy-done.7 = f32[1,128,2]{1,2,0:T(2,128)S(1)} copy-done((f32[1,128,2]{1,2,0:T(2,128)S(1)}, f32[1,128,2]{1,2,0:T(2,128)}, u32[]{:S(2)}) %copy-start.7) | copy-done | bytes 1048
  1.3 0.1 copy-done.3
  1.4 0.0 copy-done.4
  1.4 0.0 copy-done.6
  1.4 0.0 copy-start
  1.4 0.0 copy-start.1
  1.4 0.0 copy-start.2
  1.4 0.0 copy-start.5
  1.4 0.0 copy-start.8
  1.5 5.1 %collective-permute-start.2 = (bf16[176,128]{1,0:T(8,128)(2,1)S(1)}, bf16[176,128]{1,0:T(8,128)(2,1)S(1)}, u32[]{:S(2)}, u32[]{:S(2)}) collective-permute-start(bf16[176,128]{1,0:T(8,128)(2,1)S(1)} %shard_map.113.refs_0_), channel_id=1, source_target_pairs={{0,12},{4,8},{8,4},{12,0},{1,13},{5,9},{9,5},{13,1},{2,14},{6,10},... | collective-permute-start | bytes 135176 | tf_op jit(solution)/shard_map/ppermute | solution.py:354
  6.6 0.0 collective-permute-start.1
  6.6 0.6 %collective-permute-start = (bf16[176,128]{1,0:T(8,128)(2,1)S(1)}, bf16[176,128]{1,0:T(8,128)(2,1)S(1)}, u32[]{:S(2)}, u32[]{:S(2)}) collective-permute-start(bf16[176,128]{1,0:T(8,128)(2,1)S(1)} %shard_map.113.refs_0_), channel_id=1, source_target_pairs={{0,4},{4,0},{8,12},{12,8},{1,5},{5,1},{9,13},{13,9},{2,6},{6,2},{1... | collective-permute-start | bytes 135176 | tf_op jit(solution)/shard_map/ppermute | solution.py:354
  7.2 0.0 copy-done
  7.2 0.0 copy-done.1
  7.2 0.0 copy-done.2
  7.2 0.0 copy-done.5
  7.3 0.0 copy-done.8
  7.3 2.7 %shard_map.114 = (f32[3,128]{1,0:T(4,128)S(1)}, bf16[3,256,512]{2,1,0:T(8,128)(2,1)S(1)}, bf16[3,512,128]{2,1,0:T(8,128)(2,1)S(1)}) custom-call(bf16[176,128]{1,0:T(8,128)(2,1)S(1)} %shard_map.113.refs_0_, f32[3,1,128]{2,1,0:T(1,128)S(1)} %copy-done, bf16[3,144,512]{2,1,0:T(8,128)(2,1)S(1)} %copy-done.2, bf16[3,512,512]{2,1,0:T(8,128)(2,1)S(1)} %copy-done.1, ...), custom_call_target="tpu_custom_call" | custom-call | flops 1557135360 | bytes 2015232 | tf_op jit(solution)/shard_map/pallas_call | solution.py:424
  10.0 0.0 collective-permute-done.2.refs_2_
  10.0 1.5 %collective-permute-done.1.refs_1_ = bf16[176,128]{1,0:T(8,128)(2,1)S(1)} collective-permute-done((bf16[176,128]{1,0:T(8,128)(2,1)S(1)}, bf16[176,128]{1,0:T(8,128)(2,1)S(1)}, u32[]{:S(2)}, u32[]{:S(2)}) %collective-permute-start.1) | collective-permute-done | bytes 45088 | tf_op jit(solution)/shard_map/ppermute | solution.py:354
  11.5 0.0 collective-permute-done.refs_0_
  11.5 4.8 %shard_map.115.refs_0_ = f32[12,128]{1,0:T(8,128)S(1)} custom-call(bf16[176,128]{1,0:T(8,128)(2,1)S(1)} %collective-permute-done.refs_0_, bf16[176,128]{1,0:T(8,128)(2,1)S(1)} %collective-permute-done.1.refs_1_, bf16[176,128]{1,0:T(8,128)(2,1)S(1)} %collective-permute-done.2.refs_2_, f32[3,128]{1,0:T(4,128)S(1)} %get-tuple-element.16.refs_3_, ...), custom_call_target="tpu_custom_call" | custom-call | flops 4671406080 | bytes 2015232 | tf_op jit(solution)/shard_map/pallas_call | solution.py:424
  16.3 4.0 %collective-permute-start.5 = (f32[12,128]{1,0:T(8,128)S(1)}, f32[12,128]{1,0:T(8,128)S(1)}, u32[]{:S(2)}, u32[]{:S(2)}) collective-permute-start(f32[12,128]{1,0:T(8,128)S(1)} %shard_map.115.refs_0_), channel_id=1, source_target_pairs={{0,12},{4,8},{8,4},{12,0},{1,13},{5,9},{9,5},{13,1},{2,14},{6,10},... | collective-permute-start | bytes 18440 | tf_op jit(solution)/shard_map/ppermute | solution.py:354
  20.3 0.0 collective-permute-start.4
  20.3 0.6 %collective-permute-start.3 = (f32[12,128]{1,0:T(8,128)S(1)}, f32[12,128]{1,0:T(8,128)S(1)}, u32[]{:S(2)}, u32[]{:S(2)}) collective-permute-start(f32[12,128]{1,0:T(8,128)S(1)} %shard_map.115.refs_0_), channel_id=1, source_target_pairs={{0,4},{4,0},{8,12},{12,8},{1,5},{5,1},{9,13},{13,9},{2,6},{6,2},{1... | collective-permute-start | bytes 18440 | tf_op jit(solution)/shard_map/ppermute | solution.py:354
  20.9 1.0 %collective-permute-done.5.refs_3_ = f32[12,128]{1,0:T(8,128)S(1)} collective-permute-done((f32[12,128]{1,0:T(8,128)S(1)}, f32[12,128]{1,0:T(8,128)S(1)}, u32[]{:S(2)}, u32[]{:S(2)}) %collective-permute-start.5) | collective-permute-done | bytes 6176 | tf_op jit(solution)/shard_map/ppermute | solution.py:354
  21.9 2.9 %collective-permute-done.4.refs_2_ = f32[12,128]{1,0:T(8,128)S(1)} collective-permute-done((f32[12,128]{1,0:T(8,128)S(1)}, f32[12,128]{1,0:T(8,128)S(1)}, u32[]{:S(2)}, u32[]{:S(2)}) %collective-permute-start.4) | collective-permute-done | bytes 6176 | tf_op jit(solution)/shard_map/ppermute | solution.py:354
  24.8 0.0 collective-permute-done.3.refs_1_
  24.8 0.1 shard_map.116
  24.9 0.0 collective-permute-start.8
  24.9 1.7 %collective-permute-start.7 = (f32[4,128]{1,0:T(4,128)S(1)}, f32[4,128]{1,0:T(4,128)S(1)}, u32[]{:S(2)}, u32[]{:S(2)}) collective-permute-start(f32[4,128]{1,0:T(4,128)S(1)} %get-tuple-element.20.refs_0_), channel_id=1, source_target_pairs={{0,2},{1,3},{2,0},{3,1},{4,6},{5,7},{6,4},{7,5},{8,10},{9,11},{10,... | collective-permute-start | bytes 6152 | tf_op jit(solution)/shard_map/ppermute | solution.py:354
  26.7 0.1 collective-permute-start.6
  26.8 1.1 %collective-permute-done.8.refs_3_ = f32[4,128]{1,0:T(4,128)S(1)} collective-permute-done((f32[4,128]{1,0:T(4,128)S(1)}, f32[4,128]{1,0:T(4,128)S(1)}, u32[]{:S(2)}, u32[]{:S(2)}) %collective-permute-start.8) | collective-permute-done | bytes 2080 | tf_op jit(solution)/shard_map/ppermute | solution.py:354
  27.9 0.7 %collective-permute-done.7.refs_2_ = f32[4,128]{1,0:T(4,128)S(1)} collective-permute-done((f32[4,128]{1,0:T(4,128)S(1)}, f32[4,128]{1,0:T(4,128)S(1)}, u32[]{:S(2)}, u32[]{:S(2)}) %collective-permute-start.7) | collective-permute-done | bytes 2080 | tf_op jit(solution)/shard_map/ppermute | solution.py:354
  28.6 0.0 collective-permute-done.6.refs_1_
  28.6 0.6 %shard_map.117 = (f32[3,1,128]{2,1,0:T(1,128)}, f32[1,128]{1,0:T(1,128)}, f32[1,1]{1,0:T(1,128)}) custom-call(f32[4,128]{1,0:T(4,128)S(1)} %get-tuple-element.20.refs_0_, f32[4,128]{1,0:T(4,128)S(1)} %collective-permute-done.6.refs_1_, f32[4,128]{1,0:T(4,128)S(1)} %collective-permute-done.7.refs_2_, f32[4,128]{1,0:T(4,128)S(1)} %collective-permute-done.8.refs_3_, ...), custom_call_target="tpu_custom_call" | custom-call | tf_op jit(solution)/shard_map/pallas_call | solution.py:455
  (2 shorter events, 0.1 us)
Async XLA Ops:
  0.6 0.7 %copy-start.7 = (f32[1,128,2]{1,2,0:T(2,128)S(1)}, f32[1,128,2]{1,2,0:T(2,128)}, u32[]{:S(2)}) copy-start(f32[1,128,2]{1,2,0:T(2,128)} %param.12) | copy-start | bytes 3076
  0.6 0.8 %copy-start.3 = (bf16[1,128,128]{2,1,0:T(8,128)(2,1)S(1)}, bf16[1,128,128]{2,1,0:T(8,128)(2,1)}, u32[]{:S(2)}) copy-start(bf16[1,128,128]{2,1,0:T(8,128)(2,1)} %param.11) | copy-start | bytes 98308
  0.7 0.8 %copy-start.4 = (s32[1,128,2,16]{1,3,2,0:T(8,128)S(1)}, s32[1,128,2,16]{1,3,2,0:T(8,128)}, u32[]{:S(2)}) copy-start(s32[1,128,2,16]{1,3,2,0:T(8,128)} %param.10) | copy-start | bytes 49156
  0.7 0.8 %copy-start.6 = (s32[1,128,2]{1,2,0:T(2,128)S(1)}, s32[1,128,2]{1,2,0:T(2,128)}, u32[]{:S(2)}) copy-start(s32[1,128,2]{1,2,0:T(2,128)} %param.9) | copy-start | bytes 3076
  1.4 5.8 %copy-start = (f32[3,1,128]{2,1,0:T(1,128)S(1)}, f32[3,1,128]{2,1,0:T(1,128)}, u32[]{:S(2)}) copy-start(f32[3,1,128]{2,1,0:T(1,128)} %refs_5_.4) | copy-start | bytes 4612
  1.4 5.8 %copy-start.1 = (bf16[3,512,512]{2,1,0:T(8,128)(2,1)S(1)}, bf16[3,512,512]{2,1,0:T(8,128)(2,1)}, u32[]{:S(2)}) copy-start(bf16[3,512,512]{2,1,0:T(8,128)(2,1)} %refs_5_.3) | copy-start | bytes 4718596
  1.4 5.8 %copy-start.2 = (bf16[3,144,512]{2,1,0:T(8,128)(2,1)S(1)}, bf16[3,144,512]{2,1,0:T(8,128)(2,1)}, u32[]{:S(2)}) copy-start(bf16[3,144,512]{2,1,0:T(8,128)(2,1)} %refs_2_.1) | copy-start | bytes 1327108
  1.4 5.8 %copy-start.5 = (bf16[3,4,512]{2,1,0:T(4,128)(2,1)S(1)}, bf16[3,4,512]{2,1,0:T(4,128)(2,1)}, u32[]{:S(2)}) copy-start(bf16[3,4,512]{2,1,0:T(4,128)(2,1)} %refs_4_.1) | copy-start | bytes 36868
  1.4 5.8 %copy-start.8 = (bf16[256,256]{1,0:T(8,128)(2,1)S(1)}, bf16[256,256]{1,0:T(8,128)(2,1)}, u32[]{:S(2)}) copy-start(bf16[256,256]{1,0:T(8,128)(2,1)} %constant.2.clone.refs_5_.refs_7_) | copy-start | bytes 393220
  1.5 8.5 %collective-permute-start.2 = (bf16[176,128]{1,0:T(8,128)(2,1)S(1)}, bf16[176,128]{1,0:T(8,128)(2,1)S(1)}, u32[]{:S(2)}, u32[]{:S(2)}) collective-permute-start(bf16[176,128]{1,0:T(8,128)(2,1)S(1)} %shard_map.113.refs_0_), channel_id=1, source_target_pairs={{0,12},{4,8},{8,4},{12,0},{1,13},{5,9},{9,5},{13,1},{2,14},{6,10},... | collective-permute-start | bytes 135176 | tf_op jit(solution)/shard_map/ppermute | solution.py:354
  6.6 4.9 %collective-permute-start.1 = (bf16[176,128]{1,0:T(8,128)(2,1)S(1)}, bf16[176,128]{1,0:T(8,128)(2,1)S(1)}, u32[]{:S(2)}, u32[]{:S(2)}) collective-permute-start(bf16[176,128]{1,0:T(8,128)(2,1)S(1)} %shard_map.113.refs_0_), channel_id=1, source_target_pairs={{0,8},{4,12},{8,0},{12,4},{1,9},{5,13},{9,1},{13,5},{2,10},{6,14},... | collective-permute-start | bytes 135176 | tf_op jit(solution)/shard_map/ppermute | solution.py:354
  6.6 4.9 %collective-permute-start = (bf16[176,128]{1,0:T(8,128)(2,1)S(1)}, bf16[176,128]{1,0:T(8,128)(2,1)S(1)}, u32[]{:S(2)}, u32[]{:S(2)}) collective-permute-start(bf16[176,128]{1,0:T(8,128)(2,1)S(1)} %shard_map.113.refs_0_), channel_id=1, source_target_pairs={{0,4},{4,0},{8,12},{12,8},{1,5},{5,1},{9,13},{13,9},{2,6},{6,2},{1... | collective-permute-start | bytes 135176 | tf_op jit(solution)/shard_map/ppermute | solution.py:354
  16.3 5.6 %collective-permute-start.5 = (f32[12,128]{1,0:T(8,128)S(1)}, f32[12,128]{1,0:T(8,128)S(1)}, u32[]{:S(2)}, u32[]{:S(2)}) collective-permute-start(f32[12,128]{1,0:T(8,128)S(1)} %shard_map.115.refs_0_), channel_id=1, source_target_pairs={{0,12},{4,8},{8,4},{12,0},{1,13},{5,9},{9,5},{13,1},{2,14},{6,10},... | collective-permute-start | bytes 18440 | tf_op jit(solution)/shard_map/ppermute | solution.py:354
  20.3 4.5 %collective-permute-start.4 = (f32[12,128]{1,0:T(8,128)S(1)}, f32[12,128]{1,0:T(8,128)S(1)}, u32[]{:S(2)}, u32[]{:S(2)}) collective-permute-start(f32[12,128]{1,0:T(8,128)S(1)} %shard_map.115.refs_0_), channel_id=1, source_target_pairs={{0,8},{4,12},{8,0},{12,4},{1,9},{5,13},{9,1},{13,5},{2,10},{6,14},... | collective-permute-start | bytes 18440 | tf_op jit(solution)/shard_map/ppermute | solution.py:354
  20.3 4.5 %collective-permute-start.3 = (f32[12,128]{1,0:T(8,128)S(1)}, f32[12,128]{1,0:T(8,128)S(1)}, u32[]{:S(2)}, u32[]{:S(2)}) collective-permute-start(f32[12,128]{1,0:T(8,128)S(1)} %shard_map.115.refs_0_), channel_id=1, source_target_pairs={{0,4},{4,0},{8,12},{12,8},{1,5},{5,1},{9,13},{13,9},{2,6},{6,2},{1... | collective-permute-start | bytes 18440 | tf_op jit(solution)/shard_map/ppermute | solution.py:354
  24.9 3.0 %collective-permute-start.8 = (f32[4,128]{1,0:T(4,128)S(1)}, f32[4,128]{1,0:T(4,128)S(1)}, u32[]{:S(2)}, u32[]{:S(2)}) collective-permute-start(f32[4,128]{1,0:T(4,128)S(1)} %get-tuple-element.20.refs_0_), channel_id=1, source_target_pairs={{0,3},{1,2},{2,1},{3,0},{4,7},{5,6},{6,5},{7,4},{8,11},{9,10},{10,... | collective-permute-start | bytes 6152 | tf_op jit(solution)/shard_map/ppermute | solution.py:354
  24.9 3.7 %collective-permute-start.7 = (f32[4,128]{1,0:T(4,128)S(1)}, f32[4,128]{1,0:T(4,128)S(1)}, u32[]{:S(2)}, u32[]{:S(2)}) collective-permute-start(f32[4,128]{1,0:T(4,128)S(1)} %get-tuple-element.20.refs_0_), channel_id=1, source_target_pairs={{0,2},{1,3},{2,0},{3,1},{4,6},{5,7},{6,4},{7,5},{8,10},{9,11},{10,... | collective-permute-start | bytes 6152 | tf_op jit(solution)/shard_map/ppermute | solution.py:354
  26.7 1.9 %collective-permute-start.6 = (f32[4,128]{1,0:T(4,128)S(1)}, f32[4,128]{1,0:T(4,128)S(1)}, u32[]{:S(2)}, u32[]{:S(2)}) collective-permute-start(f32[4,128]{1,0:T(4,128)S(1)} %get-tuple-element.20.refs_0_), channel_id=1, source_target_pairs={{0,1},{1,0},{2,3},{3,2},{4,5},{5,4},{6,7},{7,6},{8,9},{9,8},{10,11... | collective-permute-start | bytes 6152 | tf_op jit(solution)/shard_map/ppermute | solution.py:354

commit v2 on v0

--- a/solution.py
+++ b/solution.py
@@ -84,10 +84,11 @@
                 jnp.broadcast_to(w_out[k, c : c + 1].astype(F32), (samples, hidden))
                 for c in range(4)
             ]
-            + [jnp.zeros((128 - 4 * samples, hidden), F32)],
+            ,
             axis=0,
         )
-        last_w[k] = wide.T.astype(BF16)
+        rest = jnp.zeros((hidden, 128 - 4 * samples), F32)
+        last_w[k] = jnp.concatenate([wide.T, rest], axis=1).astype(BF16)
 
 
 def serve_kernel(own, sources, slots, tiles, *refs):

time: 29.5 us -> 28.8 us (0.976); the launches traced: 29.2 us -> 29.1 us
  waiting for transfers between devices: 6.21 us -> 4.2 us
  Pallas kernels: 9.43 us -> 11.4 us
    ppermute x9, waiting for transfers between devices: 6.21 us -> 4.2 us  [exchange(): out.append(lax.ppermute(value, axes, [(i, i ^ s) for i in range(size)]))]
    pallas_call x2, Pallas kernels: 8.66 us -> 10.6 us  [serve(): call(functools.partial(serve_kernel, own, count, slots, tiles_for(count *...]
  transfers between devices with their start and end apart: 9 -> 9, of which waited for: 5 -> 5; matrix products, arithmetic and copies ran while one was open for 0% -> 0% of each run, Pallas kernels for 10% -> 12%
where the time goes in v2:
time: 28.8 us; the launch traced here: 29.1 us
  starting transfers between devices  12.1 us (42%)
  Pallas kernels  11.4 us (40%)
  waiting for transfers between devices  4.2 us (15%)
  local copies, waits for them, and re-layouts  0.74 us (3%)
  between operations  0.74 us (3%)
    ppermute x9, starting transfers between devices, exchange(): out.append(lax.ppermute(value, axes, [(i, i ^ s) for i in range(size)]))  12.1 us
    pallas_call x2, Pallas kernels, serve(): call(functools.partial(serve_kernel, own, count, slots, tiles_for(count *...  10.6 us
    ppermute x9, waiting for transfers between devices, exchange(): out.append(lax.ppermute(value, axes, [(i, i ^ s) for i in range(size)]))  4.2 us
    unnamed x18, local copies, waits for them, and re-layouts  0.74 us
    pallas_call x1, Pallas kernels, body(): call(functools.partial(finish_kernel, columns, 3 * sources * columns * pi...  0.62 us
  transfers between devices with their start and end apart: 9, of which 5 were waited for; matrix products, arithmetic and copies ran while one was open for 0% of the time, Pallas kernels for 12%

profile of v2, /device:TPU:0, one launch (start us, length us, event | category | flops | bytes accessed | tf_op | source)
XLA Modules:
  0.0 29.1 jit_solution(8034068038676092521)
XLA Ops:
  0.6 0.0 copy-start.7
  0.6 0.0 copy-start.3
  0.7 0.0 copy-start.4
  0.7 0.0 copy-start.6
  0.7 0.6 %copy-done.7 = f32[1,128,2]{1,2,0:T(2,128)S(1)} copy-done((f32[1,128,2]{1,2,0:T(2,128)S(1)}, f32[1,128,2]{1,2,0:T(2,128)}, u32[]{:S(2)}) %copy-start.7) | copy-done | bytes 1048
  1.3 0.1 copy-done.3
  1.4 0.0 copy-done.4
  1.4 0.0 copy-done.6
  1.4 0.0 copy-start
  1.4 0.0 copy-start.1
  1.4 0.0 copy-start.2
  1.4 0.0 copy-start.5
  1.4 0.0 copy-start.8
  1.5 5.1 %collective-permute-start.2 = (bf16[176,128]{1,0:T(8,128)(2,1)S(1)}, bf16[176,128]{1,0:T(8,128)(2,1)S(1)}, u32[]{:S(2)}, u32[]{:S(2)}) collective-permute-start(bf16[176,128]{1,0:T(8,128)(2,1)S(1)} %shard_map.113.refs_0_), channel_id=1, source_target_pairs={{0,12},{4,8},{8,4},{12,0},{1,13},{5,9},{9,5},{13,1},{2,14},{6,10},... | collective-permute-start | bytes 135176 | tf_op jit(solution)/shard_map/ppermute | solution.py:356
  6.6 0.0 collective-permute-start.1
  6.6 0.6 %collective-permute-start = (bf16[176,128]{1,0:T(8,128)(2,1)S(1)}, bf16[176,128]{1,0:T(8,128)(2,1)S(1)}, u32[]{:S(2)}, u32[]{:S(2)}) collective-permute-start(bf16[176,128]{1,0:T(8,128)(2,1)S(1)} %shard_map.113.refs_0_), channel_id=1, source_target_pairs={{0,4},{4,0},{8,12},{12,8},{1,5},{5,1},{9,13},{13,9},{2,6},{6,2},{1... | collective-permute-start | bytes 135176 | tf_op jit(solution)/shard_map/ppermute | solution.py:356
  7.2 0.0 copy-done
  7.2 0.0 copy-done.1
  7.2 0.0 copy-done.2
  7.2 0.0 copy-done.5
  7.3 0.0 copy-done.8
  7.3 3.5 %shard_map.114 = (f32[3,128]{1,0:T(4,128)S(1)}, bf16[3,256,512]{2,1,0:T(8,128)(2,1)S(1)}, bf16[3,512,128]{2,1,0:T(8,128)(2,1)S(1)}) custom-call(bf16[176,128]{1,0:T(8,128)(2,1)S(1)} %shard_map.113.refs_0_, f32[3,1,128]{2,1,0:T(1,128)S(1)} %copy-done, bf16[3,144,512]{2,1,0:T(8,128)(2,1)S(1)} %copy-done.2, bf16[3,512,512]{2,1,0:T(8,128)(2,1)S(1)} %copy-done.1, ...), custom_call_target="tpu_custom_call" | custom-call | flops 1557135360 | bytes 2015232 | tf_op jit(solution)/shard_map/pallas_call | solution.py:426
  10.8 0.0 collective-permute-done.2.refs_2_
  10.8 0.7 %collective-permute-done.1.refs_1_ = bf16[176,128]{1,0:T(8,128)(2,1)S(1)} collective-permute-done((bf16[176,128]{1,0:T(8,128)(2,1)S(1)}, bf16[176,128]{1,0:T(8,128)(2,1)S(1)}, u32[]{:S(2)}, u32[]{:S(2)}) %collective-permute-start.1) | collective-permute-done | bytes 45088 | tf_op jit(solution)/shard_map/ppermute | solution.py:356
  11.5 0.0 collective-permute-done.refs_0_
  11.5 7.1 %shard_map.115.refs_0_ = f32[12,128]{1,0:T(8,128)S(1)} custom-call(bf16[176,128]{1,0:T(8,128)(2,1)S(1)} %collective-permute-done.refs_0_, bf16[176,128]{1,0:T(8,128)(2,1)S(1)} %collective-permute-done.1.refs_1_, bf16[176,128]{1,0:T(8,128)(2,1)S(1)} %collective-permute-done.2.refs_2_, f32[3,128]{1,0:T(4,128)S(1)} %get-tuple-element.14.refs_3_, ...), custom_call_target="tpu_custom_call" | custom-call | flops 4671406080 | bytes 2015232 | tf_op jit(solution)/shard_map/pallas_call | solution.py:426
  18.6 0.5 %collective-permute-start.5 = (f32[12,128]{1,0:T(8,128)S(1)}, f32[12,128]{1,0:T(8,128)S(1)}, u32[]{:S(2)}, u32[]{:S(2)}) collective-permute-start(f32[12,128]{1,0:T(8,128)S(1)} %shard_map.115.refs_0_), channel_id=1, source_target_pairs={{0,12},{4,8},{8,4},{12,0},{1,13},{5,9},{9,5},{13,1},{2,14},{6,10},... | collective-permute-start | bytes 18440 | tf_op jit(solution)/shard_map/ppermute | solution.py:356
  19.1 0.0 collective-permute-start.4
  19.1 4.0 %collective-permute-start.3 = (f32[12,128]{1,0:T(8,128)S(1)}, f32[12,128]{1,0:T(8,128)S(1)}, u32[]{:S(2)}, u32[]{:S(2)}) collective-permute-start(f32[12,128]{1,0:T(8,128)S(1)} %shard_map.115.refs_0_), channel_id=1, source_target_pairs={{0,4},{4,0},{8,12},{12,8},{1,5},{5,1},{9,13},{13,9},{2,6},{6,2},{1... | collective-permute-start | bytes 18440 | tf_op jit(solution)/shard_map/ppermute | solution.py:356
  23.1 1.1 %collective-permute-done.5.refs_3_ = f32[12,128]{1,0:T(8,128)S(1)} collective-permute-done((f32[12,128]{1,0:T(8,128)S(1)}, f32[12,128]{1,0:T(8,128)S(1)}, u32[]{:S(2)}, u32[]{:S(2)}) %collective-permute-start.5) | collective-permute-done | bytes 6176 | tf_op jit(solution)/shard_map/ppermute | solution.py:356
  24.2 0.0 collective-permute-done.4.refs_2_
  24.2 0.6 %collective-permute-done.3.refs_1_ = f32[12,128]{1,0:T(8,128)S(1)} collective-permute-done((f32[12,128]{1,0:T(8,128)S(1)}, f32[12,128]{1,0:T(8,128)S(1)}, u32[]{:S(2)}, u32[]{:S(2)}) %collective-permute-start.3) | collective-permute-done | bytes 6176 | tf_op jit(solution)/shard_map/ppermute | solution.py:356
  24.7 0.1 shard_map.116.refs_0_
  24.8 0.0 collective-permute-start.8
  24.8 1.4 %collective-permute-start.7 = (f32[7,128]{1,0:T(8,128)S(1)}, f32[7,128]{1,0:T(8,128)S(1)}, u32[]{:S(2)}, u32[]{:S(2)}) collective-permute-start(f32[7,128]{1,0:T(8,128)S(1)} %shard_map.116.refs_0_), channel_id=1, source_target_pairs={{0,2},{1,3},{2,0},{3,1},{4,6},{5,7},{6,4},{7,5},{8,10},{9,11},{10,... | collective-permute-start | bytes 10760 | tf_op jit(solution)/shard_map/ppermute | solution.py:356
  26.2 0.4 %collective-permute-start.6 = (f32[7,128]{1,0:T(8,128)S(1)}, f32[7,128]{1,0:T(8,128)S(1)}, u32[]{:S(2)}, u32[]{:S(2)}) collective-permute-start(f32[7,128]{1,0:T(8,128)S(1)} %shard_map.116.refs_0_), channel_id=1, source_target_pairs={{0,1},{1,0},{2,3},{3,2},{4,5},{5,4},{6,7},{7,6},{8,9},{9,8},{10,11... | collective-permute-start | bytes 10760 | tf_op jit(solution)/shard_map/ppermute | solution.py:356
  26.7 1.2 %collective-permute-done.8.refs_3_ = f32[7,128]{1,0:T(8,128)S(1)} collective-permute-done((f32[7,128]{1,0:T(8,128)S(1)}, f32[7,128]{1,0:T(8,128)S(1)}, u32[]{:S(2)}, u32[]{:S(2)}) %collective-permute-start.8) | collective-permute-done | bytes 3616 | tf_op jit(solution)/shard_map/ppermute | solution.py:356
  27.9 0.7 %collective-permute-done.7.refs_2_ = f32[7,128]{1,0:T(8,128)S(1)} collective-permute-done((f32[7,128]{1,0:T(8,128)S(1)}, f32[7,128]{1,0:T(8,128)S(1)}, u32[]{:S(2)}, u32[]{:S(2)}) %collective-permute-start.7) | collective-permute-done | bytes 3616 | tf_op jit(solution)/shard_map/ppermute | solution.py:356
  28.5 0.0 collective-permute-done.6.refs_1_
  28.5 0.6 %shard_map.117 = (f32[3,1,128]{2,1,0:T(1,128)}, f32[1,128]{1,0:T(1,128)}, f32[1,1]{1,0:T(1,128)}) custom-call(f32[7,128]{1,0:T(8,128)S(1)} %shard_map.116.refs_0_, f32[7,128]{1,0:T(8,128)S(1)} %collective-permute-done.6.refs_1_, f32[7,128]{1,0:T(8,128)S(1)} %collective-permute-done.7.refs_2_, f32[7,128]{1,0:T(8,128)S(1)} %collective-permute-done.8.refs_3_, ...), custom_call_target="tpu_custom_call" | custom-call | tf_op jit(solution)/shard_map/pallas_call | solution.py:454
  (2 shorter events, 0.1 us)
Async XLA Ops:
  0.6 0.7 %copy-start.7 = (f32[1,128,2]{1,2,0:T(2,128)S(1)}, f32[1,128,2]{1,2,0:T(2,128)}, u32[]{:S(2)}) copy-start(f32[1,128,2]{1,2,0:T(2,128)} %param.12) | copy-start | bytes 3076
  0.6 0.8 %copy-start.3 = (bf16[1,128,128]{2,1,0:T(8,128)(2,1)S(1)}, bf16[1,128,128]{2,1,0:T(8,128)(2,1)}, u32[]{:S(2)}) copy-start(bf16[1,128,128]{2,1,0:T(8,128)(2,1)} %param.11) | copy-start | bytes 98308
  0.7 0.8 %copy-start.4 = (s32[1,128,2,16]{1,3,2,0:T(8,128)S(1)}, s32[1,128,2,16]{1,3,2,0:T(8,128)}, u32[]{:S(2)}) copy-start(s32[1,128,2,16]{1,3,2,0:T(8,128)} %param.10) | copy-start | bytes 49156
  0.7 0.8 %copy-start.6 = (s32[1,128,2]{1,2,0:T(2,128)S(1)}, s32[1,128,2]{1,2,0:T(2,128)}, u32[]{:S(2)}) copy-start(s32[1,128,2]{1,2,0:T(2,128)} %param.9) | copy-start | bytes 3076
  1.4 5.8 %copy-start = (f32[3,1,128]{2,1,0:T(1,128)S(1)}, f32[3,1,128]{2,1,0:T(1,128)}, u32[]{:S(2)}) copy-start(f32[3,1,128]{2,1,0:T(1,128)} %refs_4_.3) | copy-start | bytes 4612
  1.4 5.8 %copy-start.1 = (bf16[3,512,512]{2,1,0:T(8,128)(2,1)S(1)}, bf16[3,512,512]{2,1,0:T(8,128)(2,1)}, u32[]{:S(2)}) copy-start(bf16[3,512,512]{2,1,0:T(8,128)(2,1)} %refs_5_.2) | copy-start | bytes 4718596
  1.4 5.8 %copy-start.2 = (bf16[3,144,512]{2,1,0:T(8,128)(2,1)S(1)}, bf16[3,144,512]{2,1,0:T(8,128)(2,1)}, u32[]{:S(2)}) copy-start(bf16[3,144,512]{2,1,0:T(8,128)(2,1)} %refs_2_.1) | copy-start | bytes 1327108
  1.4 5.8 %copy-start.5 = (bf16[3,4,512]{2,1,0:T(4,128)(2,1)S(1)}, bf16[3,4,512]{2,1,0:T(4,128)(2,1)}, u32[]{:S(2)}) copy-start(bf16[3,4,512]{2,1,0:T(4,128)(2,1)} %refs_4_.2) | copy-start | bytes 36868
  1.4 5.8 %copy-start.8 = (bf16[256,256]{1,0:T(8,128)(2,1)S(1)}, bf16[256,256]{1,0:T(8,128)(2,1)}, u32[]{:S(2)}) copy-start(bf16[256,256]{1,0:T(8,128)(2,1)} %constant.2.clone.refs_5_.refs_7_) | copy-start | bytes 393220
  1.5 9.3 %collective-permute-start.2 = (bf16[176,128]{1,0:T(8,128)(2,1)S(1)}, bf16[176,128]{1,0:T(8,128)(2,1)S(1)}, u32[]{:S(2)}, u32[]{:S(2)}) collective-permute-start(bf16[176,128]{1,0:T(8,128)(2,1)S(1)} %shard_map.113.refs_0_), channel_id=1, source_target_pairs={{0,12},{4,8},{8,4},{12,0},{1,13},{5,9},{9,5},{13,1},{2,14},{6,10},... | collective-permute-start | bytes 135176 | tf_op jit(solution)/shard_map/ppermute | solution.py:356
  6.6 4.9 %collective-permute-start.1 = (bf16[176,128]{1,0:T(8,128)(2,1)S(1)}, bf16[176,128]{1,0:T(8,128)(2,1)S(1)}, u32[]{:S(2)}, u32[]{:S(2)}) collective-permute-start(bf16[176,128]{1,0:T(8,128)(2,1)S(1)} %shard_map.113.refs_0_), channel_id=1, source_target_pairs={{0,8},{4,12},{8,0},{12,4},{1,9},{5,13},{9,1},{13,5},{2,10},{6,14},... | collective-permute-start | bytes 135176 | tf_op jit(solution)/shard_map/ppermute | solution.py:356
  6.6 4.9 %collective-permute-start = (bf16[176,128]{1,0:T(8,128)(2,1)S(1)}, bf16[176,128]{1,0:T(8,128)(2,1)S(1)}, u32[]{:S(2)}, u32[]{:S(2)}) collective-permute-start(bf16[176,128]{1,0:T(8,128)(2,1)S(1)} %shard_map.113.refs_0_), channel_id=1, source_target_pairs={{0,4},{4,0},{8,12},{12,8},{1,5},{5,1},{9,13},{13,9},{2,6},{6,2},{1... | collective-permute-start | bytes 135176 | tf_op jit(solution)/shard_map/ppermute | solution.py:356
  18.6 5.5 %collective-permute-start.5 = (f32[12,128]{1,0:T(8,128)S(1)}, f32[12,128]{1,0:T(8,128)S(1)}, u32[]{:S(2)}, u32[]{:S(2)}) collective-permute-start(f32[12,128]{1,0:T(8,128)S(1)} %shard_map.115.refs_0_), channel_id=1, source_target_pairs={{0,12},{4,8},{8,4},{12,0},{1,13},{5,9},{9,5},{13,1},{2,14},{6,10},... | collective-permute-start | bytes 18440 | tf_op jit(solution)/shard_map/ppermute | solution.py:356
  19.1 5.0 %collective-permute-start.4 = (f32[12,128]{1,0:T(8,128)S(1)}, f32[12,128]{1,0:T(8,128)S(1)}, u32[]{:S(2)}, u32[]{:S(2)}) collective-permute-start(f32[12,128]{1,0:T(8,128)S(1)} %shard_map.115.refs_0_), channel_id=1, source_target_pairs={{0,8},{4,12},{8,0},{12,4},{1,9},{5,13},{9,1},{13,5},{2,10},{6,14},... | collective-permute-start | bytes 18440 | tf_op jit(solution)/shard_map/ppermute | solution.py:356
  19.1 5.6 %collective-permute-start.3 = (f32[12,128]{1,0:T(8,128)S(1)}, f32[12,128]{1,0:T(8,128)S(1)}, u32[]{:S(2)}, u32[]{:S(2)}) collective-permute-start(f32[12,128]{1,0:T(8,128)S(1)} %shard_map.115.refs_0_), channel_id=1, source_target_pairs={{0,4},{4,0},{8,12},{12,8},{1,5},{5,1},{9,13},{13,9},{2,6},{6,2},{1... | collective-permute-start | bytes 18440 | tf_op jit(solution)/shard_map/ppermute | solution.py:356
  24.8 3.0 %collective-permute-start.8 = (f32[7,128]{1,0:T(8,128)S(1)}, f32[7,128]{1,0:T(8,128)S(1)}, u32[]{:S(2)}, u32[]{:S(2)}) collective-permute-start(f32[7,128]{1,0:T(8,128)S(1)} %shard_map.116.refs_0_), channel_id=1, source_target_pairs={{0,3},{1,2},{2,1},{3,0},{4,7},{5,6},{6,5},{7,4},{8,11},{9,10},{10,... | collective-permute-start | bytes 10760 | tf_op jit(solution)/shard_map/ppermute | solution.py:356
  24.8 3.7 %collective-permute-start.7 = (f32[7,128]{1,0:T(8,128)S(1)}, f32[7,128]{1,0:T(8,128)S(1)}, u32[]{:S(2)}, u32[]{:S(2)}) collective-permute-start(f32[7,128]{1,0:T(8,128)S(1)} %shard_map.116.refs_0_), channel_id=1, source_target_pairs={{0,2},{1,3},{2,0},{3,1},{4,6},{5,7},{6,4},{7,5},{8,10},{9,11},{10,... | collective-permute-start | bytes 10760 | tf_op jit(solution)/shard_map/ppermute | solution.py:356
  26.2 2.3 %collective-permute-start.6 = (f32[7,128]{1,0:T(8,128)S(1)}, f32[7,128]{1,0:T(8,128)S(1)}, u32[]{:S(2)}, u32[]{:S(2)}) collective-permute-start(f32[7,128]{1,0:T(8,128)S(1)} %shard_map.116.refs_0_), channel_id=1, source_target_pairs={{0,1},{1,0},{2,3},{3,2},{4,5},{5,4},{6,7},{7,6},{8,9},{9,8},{10,11... | collective-permute-start | bytes 10760 | tf_op jit(solution)/shard_map/ppermute | solution.py:356
